TPU v7x, 32 devices: a whole 2x2x4 slice. The times are simulated.
32 devices in a mesh: design: 2 (over y), cluster: 4 (over z), blk: 2 (over x), sub: 2 (over core).
Axes of the slice: x: 2, y: 2, z: 4, core: 2. Of those that a mesh axis runs over, the one named last changes fastest.
Arguments:
- density: bfloat16 [16, 256, 256], P(('design', 'cluster')), parts along dimension 0, may hold values from -6 to 6
- far_cols: int32 [256], P(('design', 'cluster', 'blk', 'sub')), parts along dimension 0, may hold values from 0 to 1
- far_bucket: int32 [256], P(('design', 'cluster', 'blk', 'sub')), parts along dimension 0, may hold values from 0 to 4
- far_v: bfloat16 [256, 64, 256], P(('design', 'cluster', 'blk', 'sub')), parts along dimension 0, may hold values from -0.375 to 0.375
- far_u: bfloat16 [256, 64, 256], P(('design', 'cluster', 'blk', 'sub')), parts along dimension 0, may hold values from -0.1875 to 0.1875
- near_rows: int32 [64], P(('design', 'cluster', 'blk', 'sub')), parts along dimension 0, may hold values from 0 to 1
- near_cols: int32 [64], P(('design', 'cluster', 'blk', 'sub')), parts along dimension 0, may hold values from 0 to 5
- near_tiles: bfloat16 [64, 256, 256], P(('design', 'cluster', 'blk', 'sub')), parts along dimension 0, may hold values from -0.125 to 0.125
- ag_leaf: int32 [8192], P(('design', 'cluster', 'blk', 'sub')), parts along dimension 0, may hold values from 0 to 1
- ag_grad: bfloat16 [8192, 3, 256], P(('design', 'cluster', 'blk', 'sub')), parts along dimension 0, may hold values from -0.375 to 0.375
- ag_normal: float32 [6, 4096], P('design', ('cluster', 'blk', 'sub')), parts along dimension 0, may hold values from -5 to 5
- ag_arm: float32 [6, 4096], P('design', ('cluster', 'blk', 'sub')), parts along dimension 0, may hold values from -5 to 5
- ag_area: float32 [8192], P(('design', 'cluster', 'blk', 'sub')), parts along dimension 0, may hold values from 0.002 to 0.02
Outputs:
- potential: bfloat16 [16, 256, 256], P(('design', 'cluster')), parts along dimension 0
- sector_force: float32 [16, 3, 256], P(('design', 'cluster')), parts along dimension 0
- torque: float32 [6, 256], P('design'), parts along dimension 0
There are 2 independent parts, one for each index of `design`. A program takes and returns all parts, laid end to end along the dimension named above; each array names one. Nothing has to cross between parts.
All inputs are finite; a program needn't handle non-finite values.
Results may differ from a plain program's by a relative error of at most 0.0066.
Values may be sent and summed in bfloat16 or wider, within the bound.
A program may use at most 64 MiB of HBM per device.

v0:
```python
import math
import jax
import jax.numpy as jnp
from jax import lax
from jax.sharding import PartitionSpec as P


def padded(block, sides, width):
    for axis, dim in sides:
        count = lax.axis_size(axis)
        forward = [(i, i + 1) for i in range(count - 1)]
        forward.append((count - 1, 0))
        backward = [(target, source) for source, target in forward]
        low = lax.ppermute(
            lax.slice_in_dim(block, block.shape[dim] - width, None, axis=dim), axis, forward
        )
        high = lax.ppermute(lax.slice_in_dim(block, 0, width, axis=dim), axis, backward)
        block = jnp.concatenate([low, block, high], axis=dim)
    return block


def rank_table(bucket, rank_dim):
    widths = rank_dim // jnp.left_shift(jnp.int32(1), 4 - bucket) * (bucket > 0).astype(jnp.int32)
    return jnp.arange(rank_dim, dtype=jnp.int32)[None, :] < widths[:, None]


def surface_stress(phi_local, leaf_ids, grad_rows, normals, arms, areas):
    groups, panels, loads = phi_local.shape
    count = leaf_ids.shape[0]
    field_h = jnp.zeros((count, 3, loads), jnp.float32)
    for leaf_idx in range(groups):
        values = jnp.dot(
            grad_rows.reshape(count * 3, panels),
            phi_local[leaf_idx],
            preferred_element_type=jnp.float32,
        )
        field_h = field_h + jnp.where(
            (leaf_ids == leaf_idx)[:, None, None], values.reshape(count, 3, loads), 0.0
        )
    normal_t = jnp.transpose(normals)[:, :, None]
    along = jnp.sum(field_h * normal_t, axis=1)
    squared = jnp.sum(field_h * field_h, axis=1)
    traction = along[:, None, :] * field_h - 0.5 * squared[:, None, :] * normal_t
    weighted = traction * areas[:, None, None]
    sectors = jnp.stack(
        [
            jnp.sum(jnp.where((leaf_ids == leaf_idx)[:, None, None], weighted, 0.0), axis=0)
            for leaf_idx in range(groups)
        ]
    )
    arm_t = jnp.transpose(arms)[:, :, None]
    moment_x = jnp.sum(arm_t[:, 1] * weighted[:, 2] - arm_t[:, 2] * weighted[:, 1], axis=0)
    moment_y = jnp.sum(arm_t[:, 2] * weighted[:, 0] - arm_t[:, 0] * weighted[:, 2], axis=0)
    moment_z = jnp.sum(arm_t[:, 0] * weighted[:, 1] - arm_t[:, 1] * weighted[:, 0], axis=0)
    return (sectors, jnp.stack([moment_x, moment_y, moment_z]))


def far_field(field, far_cols, far_bucket, far_v, far_u):
    owners = lax.axis_size("cluster")
    groups, panels, loads = field.shape
    rank_dim = far_v.shape[1]
    picked = jnp.take(field, far_cols, axis=0)
    coeffs = jnp.einsum("srl,sln->srn", far_v, picked, preferred_element_type=jnp.float32)
    coeffs = jnp.where(rank_table(far_bucket, rank_dim)[:, :, None], coeffs, 0.0).astype(
        jnp.bfloat16
    )
    coeffs = coeffs.reshape(owners, groups, rank_dim, loads)
    basis = far_u.reshape(owners, groups, rank_dim, panels)
    arrived = lax.all_to_all(coeffs, "cluster", split_axis=0, concat_axis=0, tiled=True)
    return jnp.einsum("bqrl,bqrn->qln", basis, arrived, preferred_element_type=jnp.float32)


def near_field(field, near_rows, near_cols, near_tiles):
    groups = field.shape[0]
    extended = padded(field, (("cluster", 0),), groups)
    picked = jnp.take(extended, near_cols, axis=0)
    values = jnp.einsum("kij,kjn->kin", near_tiles, picked, preferred_element_type=jnp.float32)
    onehot = near_rows[:, None] == jnp.arange(groups, dtype=jnp.int32)[None, :]
    return jnp.sum(jnp.where(onehot[:, :, None, None], values[:, None], 0.0), axis=0)


def apply_operator(field, far_cols, far_bucket, far_v, far_u, near_rows, near_cols, near_tiles):
    partial_sum = far_field(field, far_cols, far_bucket, far_v, far_u) + near_field(
        field, near_rows, near_cols, near_tiles
    )
    summed = lax.psum(partial_sum, ("blk", "sub"))
    return (0.5 * field.astype(jnp.float32) + summed).astype(jnp.bfloat16)


def per_device(
    density,
    far_cols,
    far_bucket,
    far_v,
    far_u,
    near_rows,
    near_cols,
    near_tiles,
    ag_leaf,
    ag_grad,
    ag_normal,
    ag_arm,
    ag_area,
):
    first = apply_operator(
        density, far_cols, far_bucket, far_v, far_u, near_rows, near_cols, near_tiles
    )
    potential = apply_operator(
        first, far_cols, far_bucket, far_v, far_u, near_rows, near_cols, near_tiles
    )
    sector_part, torque_part = surface_stress(
        potential, ag_leaf, ag_grad, ag_normal, ag_arm, ag_area
    )
    scale = 1.0 / math.sqrt(lax.axis_size("cluster") * lax.axis_size("blk") * lax.axis_size("sub"))
    sector_force = lax.psum(sector_part, ("blk", "sub"))
    torque = lax.psum(torque_part, ("cluster", "blk", "sub"))
    return (potential, sector_force, torque * scale)


def solution(mesh):
    placed = (
        P(("design", "cluster"), None, None),
        P(("design", "cluster", "blk", "sub")),
        P(("design", "cluster", "blk", "sub")),
        P(("design", "cluster", "blk", "sub"), None, None),
        P(("design", "cluster", "blk", "sub"), None, None),
        P(("design", "cluster", "blk", "sub")),
        P(("design", "cluster", "blk", "sub")),
        P(("design", "cluster", "blk", "sub"), None, None),
        P(("design", "cluster", "blk", "sub")),
        P(("design", "cluster", "blk", "sub"), None, None),
        P("design", ("cluster", "blk", "sub")),
        P("design", ("cluster", "blk", "sub")),
        P(("design", "cluster", "blk", "sub")),
    )
    return jax.shard_map(
        per_device,
        mesh=mesh,
        in_specs=placed,
        out_specs=(
            P(("design", "cluster"), None, None),
            P(("design", "cluster"), None, None),
            P("design", None),
        ),
        check_vma=False,
    )
```

profile of v0, /device:TPU:0, one launch (start us, length us, event | category | flops | bytes accessed | tf_op | source)
XLA Modules:
  0.0 175.1 jit_solution(4676703497687636807)
XLA Ops:
  7.2 3.1 %collective-permute-start = (bf16[2,256,256]{2,1,0:T(8,128)(2,1)}, bf16[2,256,256]{2,1,0:T(8,128)(2,1)S(1)}, u32[]{:S(2)}, u32[]{:S(2)}) collective-permute-start(bf16[2,256,256]{2,1,0:T(8,128)(2,1)} %param.17), channel_id=1, source_target_pairs={{0,4},{4,8},{8,12},{12,0},{1,5},{5,9},{9,13},{13,1},{2,6},{6,10},{... | collective-permute-start | bytes 786440 | tf_op jit(solution)/shard_map/ppermute | solution.py:14
  10.3 2.1 %collective-permute-start.1 = (bf16[2,256,256]{2,1,0:T(8,128)(2,1)}, bf16[2,256,256]{2,1,0:T(8,128)(2,1)S(1)}, u32[]{:S(2)}, u32[]{:S(2)}) collective-permute-start(bf16[2,256,256]{2,1,0:T(8,128)(2,1)} %param.17), channel_id=1, source_target_pairs={{4,0},{8,4},{12,8},{0,12},{5,1},{9,5},{13,9},{1,13},{6,2},{10,6},{... | collective-permute-start | bytes 786440 | tf_op jit(solution)/shard_map/ppermute | solution.py:17
  12.4 0.7 compare_select_fusion.1
  13.1 1.6 gather_fusion
  14.9 1.1 fusion.12
  16.0 3.5 %all-to-all-start = ((bf16[4,2,64,256]{3,2,1,0:T(8,128)(2,1)}), bf16[4,2,64,256]{3,2,1,0:T(8,128)(2,1)S(1)}, u32[]{:S(2)}, u32[]{:S(2)}) async-start(bf16[4,2,64,256]{3,2,1,0:T(8,128)(2,1)} %bitcast.1), calls=%async_computation | async-start | bytes 524288 | tf_op jit(solution)/shard_map/all_to_all | solution.py:69
  19.7 0.6 copy-done.12
  20.4 4.9 %collective-permute-done.1 = bf16[2,256,256]{2,1,0:T(8,128)(2,1)S(1)} collective-permute-done((bf16[2,256,256]{2,1,0:T(8,128)(2,1)}, bf16[2,256,256]{2,1,0:T(8,128)(2,1)S(1)}, u32[]{:S(2)}, u32[]{:S(2)}) %collective-permute-start.1) | collective-permute-done | bytes 262176 | tf_op jit(solution)/shard_map/ppermute | solution.py:17
  25.4 0.6 gather_fusion.1
  26.0 0.4 copy-done.2
  26.4 0.3 convolution_bitcast_fusion.4
  27.3 2.8 %all-to-all-done = bf16[4,2,64,256]{3,2,1,0:T(8,128)(2,1)S(1)} async-done(((bf16[4,2,64,256]{3,2,1,0:T(8,128)(2,1)}), bf16[4,2,64,256]{3,2,1,0:T(8,128)(2,1)S(1)}, u32[]{:S(2)}, u32[]{:S(2)}) %all-to-all-start) | async-done | bytes 262176 | tf_op jit(solution)/shard_map/all_to_all | solution.py:69
  30.0 1.1 fusion.9
  31.3 32.5 %all-reduce.3.cloned.1.call-done = f32[2,256,256]{1,2,0:T(8,128)} async-done(((f32[2,256,256]{1,2,0:T(8,128)}), f32[2,256,256]{1,2,0:T(8,128)}) %all-reduce.3.cloned.1.call-update) | async-done | bytes 524304 | tf_op jit(solution)/shard_map/psum | solution.py:86
  63.8 1.1 add_convert_fusion.1
  64.9 1.5 collective-permute-start.2
  66.4 2.3 %collective-permute-start.3 = (bf16[2,256,256]{1,2,0:T(8,128)(2,1)S(1)}, bf16[2,256,256]{1,2,0:T(8,128)(2,1)S(1)}, u32[]{:S(2)}, u32[]{:S(2)}) collective-permute-start(bf16[2,256,256]{1,2,0:T(8,128)(2,1)S(1)} %add_convert_fusion.1), channel_id=1, source_target_pairs={{4,0},{8,4},{12,8},{0,12},{5,1},{9,5},{13,9},{1,13},{6,2},{10,6},{... | collective-permute-start | bytes 786440 | tf_op jit(solution)/shard_map/ppermute | solution.py:17
  68.7 0.6 gather_fusion.2
  69.4 1.2 fusion.11
  70.6 3.4 %all-to-all-start.1 = ((bf16[4,2,64,256]{3,2,1,0:T(8,128)(2,1)}), bf16[4,2,64,256]{3,2,1,0:T(8,128)(2,1)S(1)}, u32[]{:S(2)}, u32[]{:S(2)}) async-start(bf16[4,2,64,256]{3,2,1,0:T(8,128)(2,1)} %bitcast.7), calls=%async_computation.1 | async-start | bytes 524288 | tf_op jit(solution)/shard_map/all_to_all | solution.py:69
  74.0 1.9 %collective-permute-done.2 = bf16[2,256,256]{1,2,0:T(8,128)(2,1)S(1)} collective-permute-done((bf16[2,256,256]{1,2,0:T(8,128)(2,1)S(1)}, bf16[2,256,256]{1,2,0:T(8,128)(2,1)S(1)}, u32[]{:S(2)}, u32[]{:S(2)}) %collective-permute-start.2) | collective-permute-done | bytes 262176 | tf_op jit(solution)/shard_map/ppermute | solution.py:14
  76.0 4.2 %collective-permute-done.3 = bf16[2,256,256]{1,2,0:T(8,128)(2,1)S(1)} collective-permute-done((bf16[2,256,256]{1,2,0:T(8,128)(2,1)S(1)}, bf16[2,256,256]{1,2,0:T(8,128)(2,1)S(1)}, u32[]{:S(2)}, u32[]{:S(2)}) %collective-permute-start.3) | collective-permute-done | bytes 262176 | tf_op jit(solution)/shard_map/ppermute | solution.py:17
  80.3 0.6 gather_fusion.3
  80.8 0.3 convolution_bitcast_fusion.2
  81.7 3.2 %all-to-all-done.1 = bf16[4,2,64,256]{3,2,1,0:T(8,128)(2,1)S(1)} async-done(((bf16[4,2,64,256]{3,2,1,0:T(8,128)(2,1)}), bf16[4,2,64,256]{3,2,1,0:T(8,128)(2,1)S(1)}, u32[]{:S(2)}, u32[]{:S(2)}) %all-to-all-start.1) | async-done | bytes 262176 | tf_op jit(solution)/shard_map/all_to_all | solution.py:69
  84.9 1.1 fusion.10
  86.0 0.7 copy-done.6
  86.7 0.3 copy-done.3
  87.0 0.3 copy.72
  87.3 0.3 reshape.95
  87.7 0.3 copy-done.4
  88.1 0.5 copy-done.5
  88.7 29.0 %all-reduce.5.cloned.1.call-done = f32[2,256,256]{1,2,0:T(8,128)} async-done(((f32[2,256,256]{1,2,0:T(8,128)}), f32[2,256,256]{1,2,0:T(8,128)}) %all-reduce.5.cloned.1.call-update) | async-done | bytes 524304 | tf_op jit(solution)/shard_map/psum | solution.py:86
  117.7 1.1 add_convert_fusion
  118.8 0.3 convolution_bitcast_fusion.1
  119.1 1.2 convolution_bitcast_fusion
  120.3 0.8 copy.77
  121.4 0.3 reshape.96
  121.7 1.4 copy.74
  123.1 0.3 reshape.97
  123.5 2.9 %multiply_reduce_fusion.1 = (f32[256,256]{1,0:T(8,128)S(1)}, f32[256,3,256]{2,1,0:T(4,128)S(1)}) fusion(f32[256,3,256]{2,1,0:T(4,128)S(1)} %reshape.97, pred[256]{0:T(512)(128)(4,1)S(1)} %get-tuple-element.31, f32[256,3,256]{2,1,0:T(4,128)S(1)} %reshape.96, pred[256]{0:T(512)(128)(4,1)S(1)} %get-tuple-element.30), kind=kLoop, calls=%fused_computation.26 | loop fusion | flops 917504 | bytes 2621952 | tf_op jit(solution)/shard_map/reduce_sum | solution.py:42
  126.5 0.7 copy-done.8
  127.1 1.9 %select_reduce_fusion.1 = (f32[3,256]{1,0:T(4,128)S(1)}, f32[3,256]{1,0:T(4,128)S(1)}, f32[256,3,256]{2,1,0:T(4,128)S(1)}) fusion(pred[256]{0:T(512)(128)(4,1)S(1)} %get-tuple-element.30, pred[256]{0:T(512)(128)(4,1)S(1)} %get-tuple-element.31, f32[256]{0:T(256)S(1)} %copy-done.8, f32[256,3]{1,0:T(8,128)S(1)} %copy.75, ...), kind=kOutput, calls=%fused_computation.25 | output fusion | flops 1833474 | bytes 1845760 | tf_op jit(solution)/shard_map/mul | solution.py:43
  129.1 0.5 fusion.36
  129.8 31.3 %psum.31 = f32[3,256]{1,0:T(4,128)S(1)} all-reduce(f32[3,256]{1,0:T(4,128)S(1)} %pad_maximum_fusion.3), channel_id=1, replica_groups=mesh['design'=2,'cluster'=4,'blk'=2,'sub'=2] {'cluster','blk','sub'}, use_global_device_ids=true, to_apply=%region_12.15 | all-reduce | flops 768 | bytes 6144 | tf_op jit(solution)/shard_map/psum | solution.py:116
  161.2 0.6 broadcast_multiply_fusion.1
  161.8 5.8 %psum.30 = f32[2,3,256]{2,1,0:T(4,128)S(1)} all-reduce(f32[2,3,256]{2,1,0:T(4,128)S(1)} %pad_maximum_fusion.2), channel_id=1, replica_groups=mesh['design'=2,'cluster'=4,'blk'=2,'sub'=2] {'blk','sub'}, use_global_device_ids=true, to_apply=%region_8.11 | all-reduce | flops 1536 | bytes 12288 | tf_op jit(solution)/shard_map/psum | solution.py:115
  167.6 0.6 copy.78
  (49 shorter events, 2.5 us)
Async XLA Ops:
  7.2 22.9 %copy-start = (bf16[8,64,256]{2,1,0:T(8,128)(2,1)S(1)}, bf16[8,64,256]{2,1,0:T(8,128)(2,1)}, u32[]{:S(2)}) copy-start(bf16[8,64,256]{2,1,0:T(8,128)(2,1)} %param.21) | copy-start | bytes 786436
  7.2 5.8 %copy-start.9 = (s32[8]{0:T(128)S(1)}, s32[8]{0:T(128)}, u32[]{:S(2)}) copy-start(s32[8]{0:T(128)} %param.18) | copy-start | bytes 100
  7.2 13.2 %collective-permute-start = (bf16[2,256,256]{2,1,0:T(8,128)(2,1)}, bf16[2,256,256]{2,1,0:T(8,128)(2,1)S(1)}, u32[]{:S(2)}, u32[]{:S(2)}) collective-permute-start(bf16[2,256,256]{2,1,0:T(8,128)(2,1)} %param.17), channel_id=1, source_target_pairs={{0,4},{4,8},{8,12},{12,0},{1,5},{5,9},{9,13},{13,1},{2,6},{6,10},{... | collective-permute-start | bytes 786440 | tf_op jit(solution)/shard_map/ppermute | solution.py:14
  10.3 15.1 %collective-permute-start.1 = (bf16[2,256,256]{2,1,0:T(8,128)(2,1)}, bf16[2,256,256]{2,1,0:T(8,128)(2,1)S(1)}, u32[]{:S(2)}, u32[]{:S(2)}) collective-permute-start(bf16[2,256,256]{2,1,0:T(8,128)(2,1)} %param.17), channel_id=1, source_target_pairs={{4,0},{8,4},{12,8},{0,12},{5,1},{9,5},{13,9},{1,13},{6,2},{10,6},{... | collective-permute-start | bytes 786440 | tf_op jit(solution)/shard_map/ppermute | solution.py:17
  13.0 1.6 copy-start.10
  13.1 1.8 %copy-start.7 = (bf16[8,64,256]{2,1,0:T(8,128)(2,1)S(1)}, bf16[8,64,256]{2,1,0:T(8,128)(2,1)}, u32[]{:S(2)}) copy-start(bf16[8,64,256]{2,1,0:T(8,128)(2,1)} %param.20) | copy-start | bytes 786436
  16.0 3.6 %copy-start.11 = (s32[2]{0:T(128)S(1)}, s32[2]{0:T(128)}, u32[]{:S(2)}) copy-start(s32[2]{0:T(128)} %param.23) | copy-start | bytes 28
  16.0 9.3 %copy-start.1 = (bf16[2,256,256]{2,1,0:T(8,128)(2,1)S(1)}, bf16[2,256,256]{2,1,0:T(8,128)(2,1)}, u32[]{:S(2)}) copy-start(bf16[2,256,256]{2,1,0:T(8,128)(2,1)} %param.17) | copy-start | bytes 786436
  16.0 14.0 %all-to-all-start = ((bf16[4,2,64,256]{3,2,1,0:T(8,128)(2,1)}), bf16[4,2,64,256]{3,2,1,0:T(8,128)(2,1)S(1)}, u32[]{:S(2)}, u32[]{:S(2)}) async-start(bf16[4,2,64,256]{3,2,1,0:T(8,128)(2,1)} %bitcast.1), calls=%async_computation | async-start | bytes 524288 | tf_op jit(solution)/shard_map/all_to_all | solution.py:69
  19.6 44.2 %all-reduce.3.cloned.1.call-start = ((), (), s32[]{:S(2)}) async-start(), calls=%async_computation.2 | async-start | bytes 1048576 | tf_op jit(solution)/shard_map/psum | solution.py:86
  19.7 0.7 copy-start.12
  25.4 1.0 copy-start.2
  64.9 11.1 %collective-permute-start.2 = (bf16[2,256,256]{1,2,0:T(8,128)(2,1)S(1)}, bf16[2,256,256]{1,2,0:T(8,128)(2,1)S(1)}, u32[]{:S(2)}, u32[]{:S(2)}) collective-permute-start(bf16[2,256,256]{1,2,0:T(8,128)(2,1)S(1)} %add_convert_fusion.1), channel_id=1, source_target_pairs={{0,4},{4,8},{8,12},{12,0},{1,5},{5,9},{9,13},{13,1},{2,6},{6,10},{... | collective-permute-start | bytes 786440 | tf_op jit(solution)/shard_map/ppermute | solution.py:14
  66.4 13.8 %collective-permute-start.3 = (bf16[2,256,256]{1,2,0:T(8,128)(2,1)S(1)}, bf16[2,256,256]{1,2,0:T(8,128)(2,1)S(1)}, u32[]{:S(2)}, u32[]{:S(2)}) collective-permute-start(bf16[2,256,256]{1,2,0:T(8,128)(2,1)S(1)} %add_convert_fusion.1), channel_id=1, source_target_pairs={{4,0},{8,4},{12,8},{0,12},{5,1},{9,5},{13,9},{1,13},{6,2},{10,6},{... | collective-permute-start | bytes 786440 | tf_op jit(solution)/shard_map/ppermute | solution.py:17
  70.6 14.3 %all-to-all-start.1 = ((bf16[4,2,64,256]{3,2,1,0:T(8,128)(2,1)}), bf16[4,2,64,256]{3,2,1,0:T(8,128)(2,1)S(1)}, u32[]{:S(2)}, u32[]{:S(2)}) async-start(bf16[4,2,64,256]{3,2,1,0:T(8,128)(2,1)} %bitcast.7), calls=%async_computation.1 | async-start | bytes 524288 | tf_op jit(solution)/shard_map/all_to_all | solution.py:69
  74.0 43.7 %all-reduce.5.cloned.1.call-start = ((), (), s32[]{:S(2)}) async-start(), calls=%async_computation.3 | async-start | bytes 1048576 | tf_op jit(solution)/shard_map/psum | solution.py:86
  86.0 1.0 copy-start.3
  86.0 0.7 copy-start.6
  87.3 0.7 copy-start.4
  88.0 0.7 copy-start.5
  126.4 0.7 copy-start.8
Sparse Core Ops, SparseCore 0:
  31.3 32.4 all-reduce.2
  86.1 31.5 all-reduce.4
where the time goes:
time: 176 us; the launch traced here: 175 us
  waiting for transfers between devices  78.5 us (45%)
  blocking collectives  37.2 us (21%)
  starting transfers between devices  16.1 us (9%)
  between operations  14.4 us (8%)
  local copies, waits for them, and re-layouts  13 us (7%)
  other arithmetic  9.29 us (5%)
  matrix products  6.61 us (4%)
    psum x2, waiting for transfers between devices, apply_operator(): summed = lax.psum(partial_sum, ('blk', 'sub'))  61.5 us
    psum x1, blocking collectives, per_device(): torque = lax.psum(torque_part, ('cluster', 'blk', 'sub'))  31.3 us
    ppermute x2, waiting for transfers between devices, padded(): lax.ppermute(lax.slice_in_dim(block, 0, width, axis=dim), axis, backward)  9.12 us
    all_to_all x2, starting transfers between devices, far_field(): lax.all_to_all(coeffs, 'cluster', split_axis=0, concat_axis=0, tiled=True)  6.95 us
    all_to_all x2, waiting for transfers between devices, far_field(): lax.all_to_all(coeffs, 'cluster', split_axis=0, concat_axis=0, tiled=True)  5.97 us
    psum x1, blocking collectives, per_device(): sector_force = lax.psum(sector_part, ('blk', 'sub'))  5.84 us
    unnamed x30, local copies, waits for them, and re-layouts  5.5 us
    ppermute x2, starting transfers between devices, padded(): lax.ppermute(lax.slice_in_dim(block, block.shape[dim] - width, None, axis...  4.62 us
  transfers between devices with their start and end apart: 8, of which 7 were waited for; matrix products, arithmetic and copies ran while one was open for 5% of the time, Pallas kernels for 0%

commit v1 on v0

--- a/solution.py
+++ b/solution.py
@@ -112,7 +112,7 @@
         potential, ag_leaf, ag_grad, ag_normal, ag_arm, ag_area
     )
     scale = 1.0 / math.sqrt(lax.axis_size("cluster") * lax.axis_size("blk") * lax.axis_size("sub"))
-    sector_force = lax.psum(sector_part, ("blk", "sub"))
+    sector_force = jnp.sum(lax.all_gather(sector_part, ("blk", "sub")), axis=0)
     torque = lax.psum(torque_part, ("cluster", "blk", "sub"))
     return (potential, sector_force, torque * scale)
 

time: 176 us -> 175 us (level)
    psum x1 -> x0, blocking collectives: 5.84 us -> none  [per_device(): sector_force = lax.psum(sector_part, ('blk', 'sub'))]
    all_gather x0 -> x1, blocking collectives: none -> 5.18 us  [per_device(): sector_force = jnp.sum(lax.all_gather(sector_part, ('blk', 'sub')), axis=0)]
where the time goes in v1:
time: 175 us; the launch traced here: 174 us
  waiting for transfers between devices  78.5 us (45%)
  blocking collectives  36.5 us (21%)
  starting transfers between devices  16.1 us (9%)
  between operations  14.4 us (8%)
  local copies, waits for them, and re-layouts  13 us (7%)
  other arithmetic  9.31 us (5%)
  matrix products  6.61 us (4%)
    psum x2, waiting for transfers between devices, apply_operator(): summed = lax.psum(partial_sum, ('blk', 'sub'))  61.5 us
    psum x1, blocking collectives, per_device(): torque = lax.psum(torque_part, ('cluster', 'blk', 'sub'))  31.3 us
    ppermute x2, waiting for transfers between devices, padded(): lax.ppermute(lax.slice_in_dim(block, 0, width, axis=dim), axis, backward)  9.12 us
    all_to_all x2, starting transfers between devices, far_field(): lax.all_to_all(coeffs, 'cluster', split_axis=0, concat_axis=0, tiled=True)  6.95 us
    all_to_all x2, waiting for transfers between devices, far_field(): lax.all_to_all(coeffs, 'cluster', split_axis=0, concat_axis=0, tiled=True)  5.97 us
    unnamed x30, local copies, waits for them, and re-layouts  5.5 us
    all_gather x1, blocking collectives, per_device(): sector_force = jnp.sum(lax.all_gather(sector_part, ('blk', 'sub')), axis=0)  5.18 us
    ppermute x2, starting transfers between devices, padded(): lax.ppermute(lax.slice_in_dim(block, block.shape[dim] - width, None, axis...  4.62 us
  transfers between devices with their start and end apart: 8, of which 7 were waited for; matrix products, arithmetic and copies ran while one was open for 5% of the time, Pallas kernels for 0%

profile of v1, /device:TPU:0, one launch (start us, length us, event | category | flops | bytes accessed | tf_op | source)
XLA Modules:
  0.0 174.4 jit_solution(17010260839504503311)
XLA Ops:
  7.2 3.1 %collective-permute-start = (bf16[2,256,256]{2,1,0:T(8,128)(2,1)}, bf16[2,256,256]{2,1,0:T(8,128)(2,1)S(1)}, u32[]{:S(2)}, u32[]{:S(2)}) collective-permute-start(bf16[2,256,256]{2,1,0:T(8,128)(2,1)} %param.17), channel_id=1, source_target_pairs={{0,4},{4,8},{8,12},{12,0},{1,5},{5,9},{9,13},{13,1},{2,6},{6,10},{... | collective-permute-start | bytes 786440 | tf_op jit(solution)/shard_map/ppermute | solution.py:14
  10.3 2.1 %collective-permute-start.1 = (bf16[2,256,256]{2,1,0:T(8,128)(2,1)}, bf16[2,256,256]{2,1,0:T(8,128)(2,1)S(1)}, u32[]{:S(2)}, u32[]{:S(2)}) collective-permute-start(bf16[2,256,256]{2,1,0:T(8,128)(2,1)} %param.17), channel_id=1, source_target_pairs={{4,0},{8,4},{12,8},{0,12},{5,1},{9,5},{13,9},{1,13},{6,2},{10,6},{... | collective-permute-start | bytes 786440 | tf_op jit(solution)/shard_map/ppermute | solution.py:17
  12.4 0.7 compare_select_fusion.1
  13.1 1.6 gather_fusion
  14.9 1.1 fusion.12
  16.0 3.5 %all-to-all-start = ((bf16[4,2,64,256]{3,2,1,0:T(8,128)(2,1)}), bf16[4,2,64,256]{3,2,1,0:T(8,128)(2,1)S(1)}, u32[]{:S(2)}, u32[]{:S(2)}) async-start(bf16[4,2,64,256]{3,2,1,0:T(8,128)(2,1)} %bitcast.1), calls=%async_computation | async-start | bytes 524288 | tf_op jit(solution)/shard_map/all_to_all | solution.py:69
  19.7 0.6 copy-done.12
  20.4 4.9 %collective-permute-done.1 = bf16[2,256,256]{2,1,0:T(8,128)(2,1)S(1)} collective-permute-done((bf16[2,256,256]{2,1,0:T(8,128)(2,1)}, bf16[2,256,256]{2,1,0:T(8,128)(2,1)S(1)}, u32[]{:S(2)}, u32[]{:S(2)}) %collective-permute-start.1) | collective-permute-done | bytes 262176 | tf_op jit(solution)/shard_map/ppermute | solution.py:17
  25.4 0.6 gather_fusion.1
  26.0 0.4 copy-done.2
  26.4 0.3 convolution_bitcast_fusion.4
  27.3 2.8 %all-to-all-done = bf16[4,2,64,256]{3,2,1,0:T(8,128)(2,1)S(1)} async-done(((bf16[4,2,64,256]{3,2,1,0:T(8,128)(2,1)}), bf16[4,2,64,256]{3,2,1,0:T(8,128)(2,1)S(1)}, u32[]{:S(2)}, u32[]{:S(2)}) %all-to-all-start) | async-done | bytes 262176 | tf_op jit(solution)/shard_map/all_to_all | solution.py:69
  30.0 1.1 fusion.9
  31.3 32.5 %all-reduce.3.cloned.1.call-done = f32[2,256,256]{1,2,0:T(8,128)} async-done(((f32[2,256,256]{1,2,0:T(8,128)}), f32[2,256,256]{1,2,0:T(8,128)}) %all-reduce.3.cloned.1.call-update) | async-done | bytes 524304 | tf_op jit(solution)/shard_map/psum | solution.py:86
  63.8 1.1 add_convert_fusion.1
  64.9 1.5 collective-permute-start.2
  66.4 2.3 %collective-permute-start.3 = (bf16[2,256,256]{1,2,0:T(8,128)(2,1)S(1)}, bf16[2,256,256]{1,2,0:T(8,128)(2,1)S(1)}, u32[]{:S(2)}, u32[]{:S(2)}) collective-permute-start(bf16[2,256,256]{1,2,0:T(8,128)(2,1)S(1)} %add_convert_fusion.1), channel_id=1, source_target_pairs={{4,0},{8,4},{12,8},{0,12},{5,1},{9,5},{13,9},{1,13},{6,2},{10,6},{... | collective-permute-start | bytes 786440 | tf_op jit(solution)/shard_map/ppermute | solution.py:17
  68.7 0.6 gather_fusion.2
  69.4 1.2 fusion.11
  70.6 3.4 %all-to-all-start.1 = ((bf16[4,2,64,256]{3,2,1,0:T(8,128)(2,1)}), bf16[4,2,64,256]{3,2,1,0:T(8,128)(2,1)S(1)}, u32[]{:S(2)}, u32[]{:S(2)}) async-start(bf16[4,2,64,256]{3,2,1,0:T(8,128)(2,1)} %bitcast.7), calls=%async_computation.1 | async-start | bytes 524288 | tf_op jit(solution)/shard_map/all_to_all | solution.py:69
  74.0 1.9 %collective-permute-done.2 = bf16[2,256,256]{1,2,0:T(8,128)(2,1)S(1)} collective-permute-done((bf16[2,256,256]{1,2,0:T(8,128)(2,1)S(1)}, bf16[2,256,256]{1,2,0:T(8,128)(2,1)S(1)}, u32[]{:S(2)}, u32[]{:S(2)}) %collective-permute-start.2) | collective-permute-done | bytes 262176 | tf_op jit(solution)/shard_map/ppermute | solution.py:14
  76.0 4.2 %collective-permute-done.3 = bf16[2,256,256]{1,2,0:T(8,128)(2,1)S(1)} collective-permute-done((bf16[2,256,256]{1,2,0:T(8,128)(2,1)S(1)}, bf16[2,256,256]{1,2,0:T(8,128)(2,1)S(1)}, u32[]{:S(2)}, u32[]{:S(2)}) %collective-permute-start.3) | collective-permute-done | bytes 262176 | tf_op jit(solution)/shard_map/ppermute | solution.py:17
  80.3 0.6 gather_fusion.3
  80.8 0.3 convolution_bitcast_fusion.2
  81.7 3.2 %all-to-all-done.1 = bf16[4,2,64,256]{3,2,1,0:T(8,128)(2,1)S(1)} async-done(((bf16[4,2,64,256]{3,2,1,0:T(8,128)(2,1)}), bf16[4,2,64,256]{3,2,1,0:T(8,128)(2,1)S(1)}, u32[]{:S(2)}, u32[]{:S(2)}) %all-to-all-start.1) | async-done | bytes 262176 | tf_op jit(solution)/shard_map/all_to_all | solution.py:69
  84.9 1.1 fusion.10
  86.0 0.7 copy-done.6
  86.7 0.3 copy-done.3
  87.0 0.3 copy.82
  87.3 0.3 reshape.95
  87.7 0.3 copy-done.4
  88.1 0.5 copy-done.5
  88.7 29.0 %all-reduce.5.cloned.1.call-done = f32[2,256,256]{1,2,0:T(8,128)} async-done(((f32[2,256,256]{1,2,0:T(8,128)}), f32[2,256,256]{1,2,0:T(8,128)}) %all-reduce.5.cloned.1.call-update) | async-done | bytes 524304 | tf_op jit(solution)/shard_map/psum | solution.py:86
  117.7 1.1 add_convert_fusion
  118.8 0.3 convolution_bitcast_fusion.1
  119.1 1.2 convolution_bitcast_fusion
  120.3 0.8 copy.87
  121.4 0.3 reshape.96
  121.7 1.4 copy.84
  123.1 0.3 reshape.97
  123.5 2.9 %multiply_reduce_fusion.1 = (f32[256,256]{1,0:T(8,128)S(1)}, f32[256,3,256]{2,1,0:T(4,128)S(1)}) fusion(f32[256,3,256]{2,1,0:T(4,128)S(1)} %reshape.97, pred[256]{0:T(512)(128)(4,1)S(1)} %get-tuple-element.34, f32[256,3,256]{2,1,0:T(4,128)S(1)} %reshape.96, pred[256]{0:T(512)(128)(4,1)S(1)} %get-tuple-element.33), kind=kLoop, calls=%fused_computation.26 | loop fusion | flops 917504 | bytes 2621952 | tf_op jit(solution)/shard_map/reduce_sum | solution.py:42
  126.5 0.7 copy-done.8
  127.1 1.9 %select_reduce_fusion.1 = (f32[3,256]{1,0:T(4,128)S(1)}, f32[3,256]{1,0:T(4,128)S(1)}, f32[256,3,256]{2,1,0:T(4,128)S(1)}) fusion(pred[256]{0:T(512)(128)(4,1)S(1)} %get-tuple-element.33, pred[256]{0:T(512)(128)(4,1)S(1)} %get-tuple-element.34, f32[256]{0:T(256)S(1)} %copy-done.8, f32[256,3]{1,0:T(8,128)S(1)} %copy.85, ...), kind=kOutput, calls=%fused_computation.25 | output fusion | flops 1833474 | bytes 1845760 | tf_op jit(solution)/shard_map/mul | solution.py:43
  129.1 0.5 fusion.36
  129.8 31.3 %psum.23 = f32[3,256]{1,0:T(4,128)S(1)} all-reduce(f32[3,256]{1,0:T(4,128)S(1)} %pad_maximum_fusion.3), channel_id=1, replica_groups=mesh['design'=2,'cluster'=4,'blk'=2,'sub'=2] {'cluster','blk','sub'}, use_global_device_ids=true, to_apply=%region_12.15 | all-reduce | flops 768 | bytes 6144 | tf_op jit(solution)/shard_map/psum | solution.py:116
  161.2 0.6 broadcast_multiply_fusion.1
  161.8 5.2 %all-gather = f32[8,3,256]{2,1,0:T(4,128)S(1)} all-gather(f32[2,3,256]{2,1,0:T(4,128)S(1)} %pad_maximum_fusion.2), channel_id=2, replica_groups=mesh['design'=2,'cluster'=4,'blk'=2,'sub'=2] {'blk','sub'}, dimensions={0}, use_global_device_ids=true | all-gather | bytes 30720 | tf_op jit(solution)/shard_map/all_gather | solution.py:115
  167.0 0.6 copy.88
  (50 shorter events, 2.5 us)
Async XLA Ops:
  7.2 22.9 %copy-start = (bf16[8,64,256]{2,1,0:T(8,128)(2,1)S(1)}, bf16[8,64,256]{2,1,0:T(8,128)(2,1)}, u32[]{:S(2)}) copy-start(bf16[8,64,256]{2,1,0:T(8,128)(2,1)} %param.21) | copy-start | bytes 786436
  7.2 5.8 %copy-start.9 = (s32[8]{0:T(128)S(1)}, s32[8]{0:T(128)}, u32[]{:S(2)}) copy-start(s32[8]{0:T(128)} %param.18) | copy-start | bytes 100
  7.2 13.2 %collective-permute-start = (bf16[2,256,256]{2,1,0:T(8,128)(2,1)}, bf16[2,256,256]{2,1,0:T(8,128)(2,1)S(1)}, u32[]{:S(2)}, u32[]{:S(2)}) collective-permute-start(bf16[2,256,256]{2,1,0:T(8,128)(2,1)} %param.17), channel_id=1, source_target_pairs={{0,4},{4,8},{8,12},{12,0},{1,5},{5,9},{9,13},{13,1},{2,6},{6,10},{... | collective-permute-start | bytes 786440 | tf_op jit(solution)/shard_map/ppermute | solution.py:14
  10.3 15.1 %collective-permute-start.1 = (bf16[2,256,256]{2,1,0:T(8,128)(2,1)}, bf16[2,256,256]{2,1,0:T(8,128)(2,1)S(1)}, u32[]{:S(2)}, u32[]{:S(2)}) collective-permute-start(bf16[2,256,256]{2,1,0:T(8,128)(2,1)} %param.17), channel_id=1, source_target_pairs={{4,0},{8,4},{12,8},{0,12},{5,1},{9,5},{13,9},{1,13},{6,2},{10,6},{... | collective-permute-start | bytes 786440 | tf_op jit(solution)/shard_map/ppermute | solution.py:17
  13.0 1.6 copy-start.10
  13.1 1.8 %copy-start.7 = (bf16[8,64,256]{2,1,0:T(8,128)(2,1)S(1)}, bf16[8,64,256]{2,1,0:T(8,128)(2,1)}, u32[]{:S(2)}) copy-start(bf16[8,64,256]{2,1,0:T(8,128)(2,1)} %param.20) | copy-start | bytes 786436
  16.0 3.6 %copy-start.11 = (s32[2]{0:T(128)S(1)}, s32[2]{0:T(128)}, u32[]{:S(2)}) copy-start(s32[2]{0:T(128)} %param.23) | copy-start | bytes 28
  16.0 9.3 %copy-start.1 = (bf16[2,256,256]{2,1,0:T(8,128)(2,1)S(1)}, bf16[2,256,256]{2,1,0:T(8,128)(2,1)}, u32[]{:S(2)}) copy-start(bf16[2,256,256]{2,1,0:T(8,128)(2,1)} %param.17) | copy-start | bytes 786436
  16.0 14.0 %all-to-all-start = ((bf16[4,2,64,256]{3,2,1,0:T(8,128)(2,1)}), bf16[4,2,64,256]{3,2,1,0:T(8,128)(2,1)S(1)}, u32[]{:S(2)}, u32[]{:S(2)}) async-start(bf16[4,2,64,256]{3,2,1,0:T(8,128)(2,1)} %bitcast.1), calls=%async_computation | async-start | bytes 524288 | tf_op jit(solution)/shard_map/all_to_all | solution.py:69
  19.6 44.2 %all-reduce.3.cloned.1.call-start = ((), (), s32[]{:S(2)}) async-start(), calls=%async_computation.2 | async-start | bytes 1048576 | tf_op jit(solution)/shard_map/psum | solution.py:86
  19.7 0.7 copy-start.12
  25.4 1.0 copy-start.2
  64.9 11.1 %collective-permute-start.2 = (bf16[2,256,256]{1,2,0:T(8,128)(2,1)S(1)}, bf16[2,256,256]{1,2,0:T(8,128)(2,1)S(1)}, u32[]{:S(2)}, u32[]{:S(2)}) collective-permute-start(bf16[2,256,256]{1,2,0:T(8,128)(2,1)S(1)} %add_convert_fusion.1), channel_id=1, source_target_pairs={{0,4},{4,8},{8,12},{12,0},{1,5},{5,9},{9,13},{13,1},{2,6},{6,10},{... | collective-permute-start | bytes 786440 | tf_op jit(solution)/shard_map/ppermute | solution.py:14
  66.4 13.8 %collective-permute-start.3 = (bf16[2,256,256]{1,2,0:T(8,128)(2,1)S(1)}, bf16[2,256,256]{1,2,0:T(8,128)(2,1)S(1)}, u32[]{:S(2)}, u32[]{:S(2)}) collective-permute-start(bf16[2,256,256]{1,2,0:T(8,128)(2,1)S(1)} %add_convert_fusion.1), channel_id=1, source_target_pairs={{4,0},{8,4},{12,8},{0,12},{5,1},{9,5},{13,9},{1,13},{6,2},{10,6},{... | collective-permute-start | bytes 786440 | tf_op jit(solution)/shard_map/ppermute | solution.py:17
  70.6 14.3 %all-to-all-start.1 = ((bf16[4,2,64,256]{3,2,1,0:T(8,128)(2,1)}), bf16[4,2,64,256]{3,2,1,0:T(8,128)(2,1)S(1)}, u32[]{:S(2)}, u32[]{:S(2)}) async-start(bf16[4,2,64,256]{3,2,1,0:T(8,128)(2,1)} %bitcast.7), calls=%async_computation.1 | async-start | bytes 524288 | tf_op jit(solution)/shard_map/all_to_all | solution.py:69
  74.0 43.7 %all-reduce.5.cloned.1.call-start = ((), (), s32[]{:S(2)}) async-start(), calls=%async_computation.3 | async-start | bytes 1048576 | tf_op jit(solution)/shard_map/psum | solution.py:86
  86.0 1.0 copy-start.3
  86.0 0.7 copy-start.6
  87.3 0.7 copy-start.4
  88.0 0.7 copy-start.5
  126.4 0.7 copy-start.8
Sparse Core Ops, SparseCore 0:
  31.3 32.4 all-reduce.2
  86.1 31.5 all-reduce.4
